TPU v7x, 32 devices: a whole 2x2x4 slice. The times are simulated.
32 devices in a mesh: groups: 1, px: 32 (over z, y, x, core).
Axes of the slice: x: 2, y: 2, z: 4, core: 2. Of those that a mesh axis runs over, the one named last changes fastest.
Arguments:
- fields: bfloat16 [9, 64, 256, 256], P('groups', 'px'), may hold values from -6 to 6
- target: bfloat16 [6, 64, 256, 256], P('groups', 'px'), may hold values from -34 to 34
- lift_weight: bfloat16 [9, 32], P('groups'), may hold values from -2 to 2
- mix_weight: bfloat16 [32, 32], P('groups'), may hold values from -1 to 1
- mix_bias: float32 [32], P('groups'), may hold values from -3 to 3
- proj_weight: bfloat16 [32, 6], P('groups'), may hold values from -1 to 1
- proj_bias: float32 [6], P('groups'), may hold values from -3 to 3
- spectral_weight: float32 [2, 512, 32, 1024], P('groups', 'px')
- first_moment: float32 [2, 512, 32, 1024], P('groups', 'px'), may hold values from -3 to 3
- second_moment: float32 [2, 512, 32, 1024], P('groups', 'px'), may hold values from 0.0001 to 0.03
Outputs:
- stress: bfloat16 [6, 64, 256, 256], P('groups', 'px')
- loss: float32 [1], P('groups')
- first_new: float32 [2, 512, 32, 1024], P('groups', 'px')
- step: float32 [2, 512, 32, 1024], P('groups', 'px')
All inputs are finite; a program needn't handle non-finite values.
Results may differ from a plain program's by a relative error of at most 0.0028.
The roundings to bfloat16 on the way count: a program that leaves them out, or rounds other values in their place, can miss the bound.
Values sent between devices are 32-bit elements; how exact they have to be, the bound alone decides.
A program may use at most 192 MiB of HBM per device.

v0:
```python
import functools
import math

import jax
import jax.numpy as jnp
import numpy as np
from jax import lax
from jax.experimental import pallas as pl
from jax.experimental.pallas import tpu as pltpu
from jax.sharding import PartitionSpec as P

beta_first = 0.9
beta_second = 0.999
adam_eps = 1e-08
bf16 = jnp.bfloat16
f32 = jnp.float32
vmem_limit = 60 * 1024 * 1024


def trig(freqs, points, length):
    angle = np.remainder(freqs[:, None] * points[None, :], length) * (2.0 * math.pi / length)
    return np.cos(angle), np.sin(angle)


def split_table(table):
    table = table.astype(np.float32)
    high = table.astype(bf16)
    low = (table - high.astype(np.float32)).astype(bf16)
    return np.stack([high, low], 0)


def signed(modes):
    index = np.arange(2 * modes)
    return np.where(index < modes, index, index - 2 * modes)


def make_tables(modes, grid_x, grid_y, grid_z):
    half = 2 * modes
    cz, sz = trig(np.arange(modes), np.arange(grid_z), grid_z)
    z_fwd = (np.concatenate([cz, -sz], 0) / math.sqrt(grid_z)).astype(np.float32).astype(bf16)
    factor = np.where(np.arange(modes) == 0, 1.0, 2.0)[:, None] / math.sqrt(grid_z)
    z_inv = split_table(np.concatenate([cz * factor, -sz * factor], 0))
    z_rep = np.concatenate([z_inv[0], z_inv[0], z_inv[1], np.zeros_like(z_inv[0])], 0)
    cy, sy = trig(signed(modes), np.arange(grid_y), grid_y)
    cy, sy = cy / math.sqrt(grid_y), sy / math.sqrt(grid_y)
    order = np.arange(half).reshape(half // 4, 4).T

    def rows(real, imag):
        return np.stack([real[order], imag[order]], 1).reshape(2 * half, -1)

    y_fwd = np.stack([split_table(rows(cy, -sy)), split_table(rows(sy, cy))], 0)
    y_inv = split_table(np.concatenate([rows(cy, -sy), rows(sy, cy)], 1))
    cx, sx = trig(signed(modes), np.arange(grid_x), grid_x)
    cx, sx = cx / math.sqrt(grid_x), sx / math.sqrt(grid_x)
    x_fwd = split_table(np.concatenate([cx, sx], 0))
    x_inv = split_table(
        np.concatenate(
            [np.concatenate([cx.T, -sx.T], 1), np.concatenate([sx.T, cx.T], 1)], 0
        )
    )
    return z_fwd, z_rep, y_fwd, y_inv, x_fwd, x_inv


def dot(a, b):
    return jnp.dot(a, b, preferred_element_type=f32)


def dot_nt(a, b):
    return lax.dot_general(a, b, (((1,), (1,)), ((), ())), preferred_element_type=f32)


def parts_of(x):
    high = x.astype(bf16)
    return high, (x - high.astype(f32)).astype(bf16)


def table_dot(table, data):
    high, low = parts_of(data)
    return dot(table[0], high) + (dot(table[1], high) + dot(table[0], low))


def forward_yz(field_ref, zs_ref, z_fwd_ref, y_fwd_ref, out_ref, plane, modes):
    chans = field_ref.shape[0]
    z_fwd = z_fwd_ref[...]

    for c in range(chans):
        zs_ref[:, c, :] = dot_nt(z_fwd, field_ref[c])
    total = None
    for part in range(2):
        data = zs_ref[pl.ds(part * modes, modes)].reshape(modes * chans, zs_ref.shape[2])
        high, low = parts_of(data)
        t_high, t_low = y_fwd_ref[part, 0], y_fwd_ref[part, 1]
        term = dot_nt(t_high, high) + (dot_nt(t_low, high) + dot_nt(t_high, low))
        total = term if total is None else total + term
    devices, _, slots, _ = out_ref.shape
    quads = slots // 2
    per = total.shape[0] // 4
    groups = per // 2
    for k in range(modes):
        piece = jnp.concatenate(
            [
                total[j * per : (j + 1) * per, k * chans : (k + 1) * chans]
                for j in range(4)
            ],
            1,
        )
        for r in range(2):
            for h in range(groups // quads):
                row = r * groups + h * quads
                out_ref[k * (groups // quads) + h, plane, r * quads : (r + 1) * quads, :] = piece[
                    row : row + quads
                ]


def lift_kernel(modes, fields_ref, lift_ref, z_fwd_ref, y_fwd_ref, out_ref, field_ref, zs_ref):
    plane = pl.program_id(0)
    grid_y, grid_z = fields_ref.shape[2:]
    chans = field_ref.shape[0]

    def step(i, carry):
        at = pl.ds(pl.multiple_of(i * 16, 16), 16)
        data = fields_ref[:, 0, at, :].reshape(-1, grid_z)
        lifted = dot(lift_ref[...], data).astype(bf16)
        field_ref[:, at, :] = lifted.reshape(chans, 16, grid_z)
        return carry

    lax.fori_loop(0, grid_y // 16, step, 0, unroll=2)
    forward_yz(field_ref, zs_ref, z_fwd_ref, y_fwd_ref, out_ref, plane, modes)


def forward_x(recv_ref, x_ref, quad):
    quads = recv_ref.shape[1] // 2
    half = x_ref.shape[1] // 2
    real = table_dot(x_ref, recv_ref[:, quad, :])
    imag = table_dot(x_ref, recv_ref[:, quads + quad, :])
    return real[:half] + imag[half:], imag[:half] - real[half:]


def lane_group(shape):
    return lax.broadcasted_iota(jnp.int32, shape, 1) // 32


def spread_rows(data):
    group = lane_group(data.shape)
    return jnp.concatenate([jnp.where(group == j, data, 0.0) for j in range(4)], 0)


def expand(data, e_ref):
    high, low = parts_of(spread_rows(data))
    return dot(high, e_ref[...]) + dot(low, e_ref[...])


def mix_kernel(recv_ref, weight_ref, x_fwd_ref, x_inv_ref, e_ref, vhat_ref, out_ref):
    quads = recv_ref.shape[1] // 2
    quad = pl.program_id(0)
    v_real, v_imag = forward_x(recv_ref, x_fwd_ref, quad)
    vhat_ref[0, 0], vhat_ref[0, 1] = v_real, v_imag
    a_real, a_imag = expand(v_real, e_ref), expand(v_imag, e_ref)
    half = v_real.shape[0]
    m_real, m_imag = None, None
    for t in range(8):
        lanes = slice(t * 128, (t + 1) * 128)
        w_real = weight_ref[0, :, :, lanes].reshape(4 * half, 128)
        w_imag = weight_ref[1, :, :, lanes].reshape(4 * half, 128)
        ar, ai = a_real[:, lanes], a_imag[:, lanes]
        pr = w_real * ar - w_imag * ai
        pi = w_real * ai + w_imag * ar
        m_real = pr if m_real is None else m_real + pr
        m_imag = pi if m_imag is None else m_imag + pi

    def gather(m):
        m = m + pltpu.roll(m, 64, 1)
        m = m + pltpu.roll(m, 32, 1)
        group = lane_group((half, 128))
        out = m[:half]
        for j in range(1, 4):
            out = jnp.where(group == j, m[j * half : (j + 1) * half], out)
        return out

    mixed = jnp.concatenate([gather(m_real), gather(m_imag)], 0)
    back = table_dot(x_inv_ref, mixed)
    grid_x = recv_ref.shape[0]
    out_ref[:, quad, :] = back[:grid_x]
    out_ref[:, quads + quad, :] = back[grid_x:]


poly = (0.254829592, -0.284496736, 1.421413741, -1.453152027, 1.061405429)
poly_p = 0.3275911


def gelu_parts(u):
    e = jnp.exp(u * u * -0.5)
    t = 1.0 / (1.0 + (poly_p / math.sqrt(2.0)) * jnp.abs(u))
    q = 0.5 * poly[4]
    for a in poly[3::-1]:
        q = q * t + 0.5 * a
    q = q * t * e
    cdf = jnp.where(u >= 0.0, 1.0 - q, q)
    return cdf, cdf + u * e * (1.0 / math.sqrt(2.0 * math.pi))


def plane_kernel(
    modes,
    recv_ref,
    fields_ref,
    target_ref,
    lift_ref,
    mix_ref,
    bias_ref,
    proj_ref,
    proj_t_ref,
    proj_bias_ref,
    z_fwd_ref,
    z_rep_ref,
    y_fwd_ref,
    y_inv_ref,
    stress_ref,
    out_ref,
    err_ref,
    field_ref,
    zs_ref,
    us_ref,
    v_ref,
):
    plane = pl.program_id(0)
    grid_y, grid_z = fields_ref.shape[2:]
    chans = field_ref.shape[0]
    comps = target_ref.shape[0]
    devices, _, slots, _ = recv_ref.shape
    quads = slots // 2
    per = 4 * modes // 4
    groups = per // 2
    halves = groups // quads
    columns = []
    for k in range(modes):
        g = jnp.concatenate(
            [
                recv_ref[k * halves + h, plane, r * quads : (r + 1) * quads, :]
                for r in range(2)
                for h in range(halves)
            ],
            0,
        )
        columns.append(
            jnp.concatenate([g[:, j * chans : (j + 1) * chans] for j in range(4)], 0)
        )
    spec = jnp.concatenate(columns, 1).T
    high, low = parts_of(spec)
    t_high, t_low = y_inv_ref[0], y_inv_ref[1]
    u = dot(high, t_high) + (dot(high, t_low) + dot(low, t_high))
    us_ref[...] = u.reshape(modes, chans, 2 * grid_y)
    for o in range(chans):
        row = us_ref[:, o, :]
        both = jnp.concatenate([row[:, :grid_y], row[:, grid_y:]], 0)
        b_high = both.astype(bf16).astype(f32)
        b_low = both - b_high
        stacked = jnp.concatenate([b_high, b_low, b_high, jnp.zeros_like(both)], 0)
        v_ref[o] = stacked.T.astype(bf16)

    def step(i, err):
        at = pl.ds(pl.multiple_of(i * 16, 16), 16)
        data = fields_ref[:, 0, at, :].reshape(-1, grid_z)
        lifted = dot(lift_ref[...], data).astype(bf16)
        spatial = dot(v_ref[:, at, :].reshape(chans * 16, -1), z_rep_ref[...])
        spatial = spatial.reshape(chans, 16, grid_z)
        target = target_ref[:, 0, at, :].astype(f32)
        stress, grads = [], []
        rows = chans * 8
        for h in range(2):
            pre = dot(mix_ref[...], lifted[h * rows : (h + 1) * rows])
            pre = pre.reshape(chans, 8, grid_z) + bias_ref[...]
            pre = pre + spatial[:, h * 8 : (h + 1) * 8]
            cdf, slope = gelu_parts(pre)
            act = (pre * cdf).astype(bf16).reshape(rows, grid_z)
            pred = dot(proj_ref[...], act).reshape(comps, 8, grid_z) + proj_bias_ref[...]
            stress.append(pred)
            error = pred - target[:, h * 8 : (h + 1) * 8]
            err = err + jnp.sum(error * error, 0)
            error_b = error.reshape(comps * 8, grid_z).astype(bf16)
            back = dot(proj_t_ref[...], error_b).reshape(chans, 8, grid_z)
            grads.append(back * slope)
        stress_ref[:, 0, at, :] = jnp.concatenate(stress, 1).astype(bf16)
        field_ref[:, at, :] = jnp.concatenate(grads, 1).astype(bf16)
        return err

    err = lax.fori_loop(0, grid_y // 16, step, jnp.zeros((8, grid_z), f32))
    folded = err[:, :128]
    for t in range(1, grid_z // 128):
        folded = folded + err[:, t * 128 : (t + 1) * 128]

    @pl.when(plane == 0)
    def _():
        err_ref[...] = folded

    @pl.when(plane > 0)
    def _():
        err_ref[...] += folded

    forward_yz(field_ref, zs_ref, z_fwd_ref, y_fwd_ref, out_ref, plane, modes)


def adam_kernel(
    recv_ref, vhat_ref, scale_ref, first_ref, second_ref, x_ref, e_ref, f_ref, first_out, step_out
):
    quad = pl.program_id(0)
    d_real, d_imag = forward_x(recv_ref, x_ref, quad)
    scale = scale_ref[0]
    b_real, b_imag = expand(d_real * scale, f_ref), expand(d_imag * scale, f_ref)
    a_real, a_imag = expand(vhat_ref[0, 0], e_ref), expand(vhat_ref[0, 1], e_ref)
    half = d_real.shape[0]
    first_corr = 1.0 / (1.0 - beta_first**2)
    second_corr = 1.0 / (1.0 - beta_second**2)
    for t in range(8):
        lanes = slice(t * 128, (t + 1) * 128)
        ar, ai = a_real[:, lanes], a_imag[:, lanes]
        grads = (ar * b_real + ai * b_imag, ar * b_imag - ai * b_real)
        for r in range(2):
            grad = grads[r].reshape(4, half, 128)
            first = beta_first * first_ref[r, :, :, lanes] + (1.0 - beta_first) * grad
            second = (
                beta_second * second_corr * second_ref[r, :, :, lanes]
                + ((1.0 - beta_second) * second_corr) * grad * grad
            )
            first_out[r, :, :, lanes] = first
            step_out[r, :, :, lanes] = first * first_corr / (jnp.sqrt(second) + adam_eps)


def exchange_kernel(axis, devices, count, *refs):
    sends, recvs = refs[:count], refs[count : 2 * count]
    send_sem, recv_sem, own_sem = refs[2 * count :]
    me = lax.axis_index(axis)
    barrier = pltpu.get_barrier_semaphore()

    def greet(off, carry):
        pl.semaphore_signal(
            barrier,
            inc=1,
            device_id={axis: lax.rem(me + off, devices)},
            device_id_type=pl.DeviceIdType.MESH,
        )
        return carry

    lax.fori_loop(1, devices, greet, 0)
    pl.semaphore_wait(barrier, devices - 1)

    def copy(i, off, there, slot):
        src = sends[i].at[there] if sends[i].shape == recvs[i].shape else sends[i]
        return pltpu.make_async_remote_copy(
            src_ref=src,
            dst_ref=recvs[i].at[slot],
            send_sem=send_sem.at[i, off],
            recv_sem=recv_sem.at[i, off],
            device_id={axis: there},
            device_id_type=pl.DeviceIdType.MESH,
        )

    def start(off, carry):
        for i in range(count):
            copy(i, off, lax.rem(me + off, devices), me).start()
        return carry

    def finish(off, carry):
        for i in range(count):
            copy(
                i, off, lax.rem(me + off, devices), lax.rem(me + devices - off, devices)
            ).wait()
        return carry

    lax.fori_loop(1, devices, start, 0)
    own = []
    for i in range(count):
        src = sends[i].at[me] if sends[i].shape == recvs[i].shape else sends[i]
        own.append(pltpu.make_async_copy(src, recvs[i].at[me], own_sem.at[i]))
        own[-1].start()
    for item in own:
        item.wait()
    lax.fori_loop(1, devices, finish, 0)


def exchange(arrays, devices, ident):
    count = len(arrays)
    shapes = [
        jax.ShapeDtypeStruct(a.shape if a.ndim == 4 else (devices,) + a.shape, a.dtype)
        for a in arrays
    ]
    return pl.pallas_call(
        functools.partial(exchange_kernel, "px", devices, count),
        out_shape=shapes,
        in_specs=[pl.BlockSpec(memory_space=pltpu.VMEM)] * count,
        out_specs=[pl.BlockSpec(memory_space=pltpu.VMEM)] * count,
        scratch_shapes=[
            pltpu.SemaphoreType.DMA((count, devices)),
            pltpu.SemaphoreType.DMA((count, devices)),
            pltpu.SemaphoreType.DMA((count,)),
        ],
        compiler_params=pltpu.CompilerParams(collective_id=ident, has_side_effects=True),
        name="exchange%d" % ident,
    )(*arrays)


def whole(shape):
    zeros = (0,) * len(shape)
    return pl.BlockSpec(tuple(shape), lambda i: zeros)


def spread(weight, size):
    eye = jnp.eye(size, dtype=weight.dtype)
    out = weight[:, None, :, None] * eye[None, :, None, :]
    return out.reshape(weight.shape[0] * size, weight.shape[1] * size)


def body(
    fields,
    target,
    lift_weight,
    mix_weight,
    mix_bias,
    proj_weight,
    proj_bias,
    spectral_weight,
    first_moment,
    second_moment,
):
    devices = lax.axis_size("px")
    rank = lax.axis_index("px")
    in_ch, planes, grid_y, grid_z = fields.shape
    chans = mix_weight.shape[0]
    comps = target.shape[0]
    half = spectral_weight.shape[2]
    modes = half // 2
    local_pairs = spectral_weight.shape[1]
    grid_x = planes * devices
    quads = local_pairs // 4
    slots = 2 * quads
    z_fwd, z_rep, y_fwd, y_inv, x_fwd, x_inv = (
        jnp.asarray(t) for t in make_tables(modes, grid_x, grid_y, grid_z)
    )
    lanes = np.arange(128) % 32
    e_table = jnp.asarray((lanes[:, None] == np.arange(1024)[None, :] // 32).astype(bf16))
    f_table = jnp.asarray((lanes[:, None] == lanes[None, :]).astype(bf16))
    chunk = (devices, planes, slots, 128)
    params = pltpu.CompilerParams(
        dimension_semantics=("arbitrary",), vmem_limit_bytes=vmem_limit
    )

    lift16 = spread(lift_weight.T, 16)
    lift_split = (
        lift16.reshape(chans, 2, 8, in_ch * 16).transpose(1, 0, 2, 3).reshape(chans * 16, -1)
    )
    mix8 = spread(mix_weight.T, 8)
    proj8 = spread(proj_weight.T, 8)
    proj8_t = spread(proj_weight, 8)

    plane_block = lambda n: pl.BlockSpec((n, 1, grid_y, grid_z), lambda p: (0, p, 0, 0))
    spectra = pl.pallas_call(
        functools.partial(lift_kernel, modes),
        grid=(planes,),
        out_shape=jax.ShapeDtypeStruct(chunk, f32),
        in_specs=[
            plane_block(in_ch),
            whole(lift16.shape),
            whole(z_fwd.shape),
            whole(y_fwd.shape),
        ],
        out_specs=whole(chunk),
        scratch_shapes=[
            pltpu.VMEM((chans, grid_y, grid_z), bf16),
            pltpu.VMEM((half, chans, grid_y), f32),
        ],
        compiler_params=params,
        name="lift_spectrum",
    )(fields, lift16, z_fwd, y_fwd)

    (moved,) = exchange([spectra], devices, 0)

    flat = (grid_x, slots, 128)
    pair_block = pl.BlockSpec((2, 4, half, 1024), lambda q: (0, q, 0, 0))
    vhat_block = pl.BlockSpec((1, 2, half, 128), lambda q: (q, 0, 0, 0))
    vhat, sending = pl.pallas_call(
        mix_kernel,
        grid=(quads,),
        out_shape=(
            jax.ShapeDtypeStruct((quads, 2, half, 128), f32),
            jax.ShapeDtypeStruct(flat, f32),
        ),
        in_specs=[
            whole(flat),
            pair_block,
            whole(x_fwd.shape),
            whole(x_inv.shape),
            whole(e_table.shape),
        ],
        out_specs=(vhat_block, whole(flat)),
        compiler_params=params,
        name="mix_modes",
    )(moved.reshape(flat), spectral_weight, x_fwd, x_inv, e_table)

    (result,) = exchange([sending.reshape(chunk)], devices, 1)

    bias = jnp.broadcast_to(mix_bias[:, None, None], (chans, 1, grid_z))
    pbias = jnp.broadcast_to(proj_bias[:, None, None], (comps, 1, grid_z))
    stress, grad_spectra, err = pl.pallas_call(
        functools.partial(plane_kernel, modes),
        grid=(planes,),
        out_shape=(
            jax.ShapeDtypeStruct(target.shape, bf16),
            jax.ShapeDtypeStruct(chunk, f32),
            jax.ShapeDtypeStruct((8, 128), f32),
        ),
        in_specs=[whole(chunk), plane_block(in_ch), plane_block(comps)]
        + [
            whole(a.shape)
            for a in (
                lift_split, mix8, bias, proj8, proj8_t, pbias, z_fwd, z_rep, y_fwd, y_inv
            )
        ],
        out_specs=(plane_block(comps), whole(chunk), whole((8, 128))),
        scratch_shapes=[
            pltpu.VMEM((chans, grid_y, grid_z), bf16),
            pltpu.VMEM((half, chans, grid_y), f32),
            pltpu.VMEM((modes, chans, 2 * grid_y), f32),
            pltpu.VMEM((chans, grid_y, 8 * modes), bf16),
        ],
        compiler_params=params,
        name="planes",
    )(
        result, fields, target, lift_split, mix8, bias, proj8, proj8_t, pbias,
        z_fwd, z_rep, y_fwd, y_inv,
    )

    grads_moved, errors = exchange([grad_spectra, err], devices, 2)
    loss = (jnp.sum(errors) / (2.0 * comps * grid_x * grid_y * grid_z)).reshape(1)

    kz_index = (rank * local_pairs + jnp.arange(local_pairs, dtype=jnp.int32)) // half
    scale = jnp.where(kz_index == 0, 1.0, 2.0).astype(f32)
    scale = jnp.repeat(scale, 32).reshape(quads, 1, 128)
    first_new, step = pl.pallas_call(
        adam_kernel,
        grid=(quads,),
        out_shape=(
            jax.ShapeDtypeStruct(first_moment.shape, f32),
            jax.ShapeDtypeStruct(first_moment.shape, f32),
        ),
        in_specs=[
            whole(flat),
            vhat_block,
            pl.BlockSpec((1, 1, 128), lambda q: (q, 0, 0)),
            pair_block,
            pair_block,
            whole(x_fwd.shape),
            whole(e_table.shape),
            whole(f_table.shape),
        ],
        out_specs=(pair_block, pair_block),
        compiler_params=params,
        name="adam",
    )(
        grads_moved.reshape(flat), vhat, scale, first_moment, second_moment,
        x_fwd, e_table, f_table,
    )
    return (stress, loss, first_new, step)


def solution(mesh):
    placed = (
        P("groups", "px", None, None),
        P("groups", "px", None, None),
        P("groups", None),
        P("groups", None),
        P("groups"),
        P("groups", None),
        P("groups"),
        P("groups", "px", None, None),
        P("groups", "px", None, None),
        P("groups", "px", None, None),
    )
    return jax.shard_map(
        body,
        mesh=mesh,
        in_specs=placed,
        out_specs=(
            P("groups", "px", None, None),
            P("groups"),
            P("groups", "px", None, None),
            P("groups", "px", None, None),
        ),
        check_vma=False,
    )
```

profile of v0, /device:TPU:15, one launch (start us, length us, event | category | flops | bytes accessed | tf_op | source)
XLA Modules:
  0.0 137.5 jit_solution(12933867781437985018)
XLA Ops:
  0.6 0.0 copy-start
  0.7 0.1 copy.30
  0.8 0.1 copy.26
  0.9 0.1 broadcast_in_dim.20
  0.9 0.7 broadcast_in_dim.38.scale_ref
  1.6 1.3 broadcast_in_dim.15.proj_bias_ref
  2.9 0.8 copy.29
  3.7 1.4 broadcast_in_dim.14.bias_ref
  5.1 0.7 mul.95
  5.8 0.1 copy.28
  5.9 0.1 mul.99
  6.0 0.7 broadcast_multiply_fusion.4
  6.7 0.8 broadcast_multiply_fusion.2
  7.5 0.5 mul.114
  8.0 0.7 copy.32.proj_t_ref
  8.7 0.8 broadcast_multiply_fusion.3
  9.5 1.1 mul.110.proj_ref
  10.6 0.0 copy-done
  10.6 0.1 broadcast_multiply_fusion.1
  10.8 1.9 %mul.94 = bf16[512,144]{0,1:T(8,128)(2,1)S(1)} reshape(bf16[32,16,9,16]{1,0,3,2:T(8,128)(2,1)S(1)} %broadcast_multiply_fusion.1) | data formatting | bytes 294912 | tf_op jit(solution)/shard_map/mul | solution.py:408
  12.7 0.8 copy.27.lift_ref
  13.5 11.3 %lift_spectrum.1.refs_0_ = f32[32,2,8,128]{3,2,1,0:T(8,128)} custom-call(bf16[9,2,256,256]{3,2,1,0:T(8,128)(2,1)} %fields_ref.3, bf16[512,144]{1,0:T(8,128)(2,1)} %copy.27.lift_ref, bf16[32,256]{1,0:T(8,128)(2,1)} %constant.50.clone.z_fwd_ref, bf16[2,2,64,256]{3,2,1,0:T(8,128)(2,1)} %constant.52.clone.y_fwd_ref), custom_call_target="tpu_custom_call" | custom-call | tf_op jit(solution)/shard_map/lift_spectrum/pallas_call | solution.py:455
  24.8 14.0 %exchange0.1 = f32[32,2,8,128]{3,2,1,0:T(8,128)} custom-call(f32[32,2,8,128]{3,2,1,0:T(8,128)} %lift_spectrum.1.refs_0_), custom_call_target="tpu_custom_call" | custom-call | tf_op jit(solution)/shard_map/exchange0/pallas_call | solution.py:386
  38.8 6.8 %mix_modes.1 = (f32[4,2,32,128]{3,2,1,0:T(8,128)}, f32[64,8,128]{2,1,0:T(8,128)}) custom-call(f32[64,8,128]{2,1,0:T(8,128)} %bitcast.21, f32[2,16,32,1024]{3,2,1,0:T(8,128)} %weight_ref.1, bf16[2,64,64]{2,1,0:T(8,128)(2,1)} %constant.54.clone.x_fwd_ref.x_ref, bf16[2,128,64]{2,1,0:T(8,128)(2,1)} %constant.55.clone.x_inv_ref, ...), custom_call_target="tpu_custom_call" | custom-call | tf_op jit(solution)/shard_map/mix_modes/pallas_call | solution.py:479
  45.6 13.5 %exchange1.1.recv_ref = f32[32,2,8,128]{3,2,1,0:T(8,128)} custom-call(f32[32,2,8,128]{3,2,1,0:T(8,128)} %bitcast.24), custom_call_target="tpu_custom_call" | custom-call | tf_op jit(solution)/shard_map/exchange1/pallas_call | solution.py:386
  59.1 0.2 broadcast_multiply_fusion
  59.3 3.5 %mul.106.mix_ref = bf16[256,256]{1,0:T(8,128)(2,1)} reshape(bf16[32,8,32,8]{3,2,1,0:T(8,128)(2,1)S(1)} %broadcast_multiply_fusion) | data formatting | bytes 262144 | tf_op jit(solution)/shard_map/mul | solution.py:408
  62.8 44.8 %planes.1 = (bf16[6,2,256,256]{3,2,1,0:T(8,128)(2,1)}, f32[32,2,8,128]{3,2,1,0:T(8,128)}, f32[8,128]{1,0:T(8,128)}) custom-call(f32[32,2,8,128]{3,2,1,0:T(8,128)} %exchange1.1.recv_ref, bf16[9,2,256,256]{3,2,1,0:T(8,128)(2,1)} %fields_ref.3, bf16[6,2,256,256]{3,2,1,0:T(8,128)(2,1)} %target_ref.1, bf16[512,144]{1,0:T(8,128)(2,1)} %bitcast.22, ...), custom_call_target="tpu_custom_call" | custom-call | tf_op jit(solution)/shard_map/planes/pallas_call | solution.py:502
  107.7 17.0 %exchange2.1 = (f32[32,2,8,128]{3,2,1,0:T(8,128)}, f32[32,8,128]{2,1,0:T(8,128)}) custom-call(f32[32,2,8,128]{3,2,1,0:T(8,128)} %get-tuple-element.15.refs_0_, f32[8,128]{1,0:T(8,128)} %get-tuple-element.16.refs_1_), custom_call_target="tpu_custom_call" | custom-call | tf_op jit(solution)/shard_map/exchange2/pallas_call | solution.py:386
  124.7 1.5 %reduce_sum.9 = f32[]{:T(128)} reduce(f32[32,8,128]{2,1,0:T(8,128)} %get-tuple-element.17, f32[]{:T(128)} %constant.38.clone.1), dimensions={0,1,2}, to_apply=%region_0.0 | reduce | flops 32767 | bytes 131080 | tf_op jit(solution)/shard_map/reduce_sum | solution.py:532
  126.9 9.4 %adam.1 = (f32[2,16,32,1024]{3,2,1,0:T(8,128)}, f32[2,16,32,1024]{3,2,1,0:T(8,128)}) custom-call(f32[64,8,128]{2,1,0:T(8,128)} %bitcast.23, f32[4,2,32,128]{3,2,1,0:T(8,128)} %get-tuple-element.19.vhat_ref, f32[4,1,128]{2,1,0:T(1,128)} %broadcast_in_dim.38.scale_ref, f32[2,16,32,1024]{3,2,1,0:T(8,128)} %first_ref.1, f32[2,16,32,1024]{3,2,1,0:T(8,128)} %second_ref.1, ...), custom_call_target="tpu_custom_call" | custom-call | tf_op jit(solution)/shard_map/adam/pallas_call | solution.py:537
  (4 shorter events, 0.1 us)
Async XLA Ops:
  0.6 10.0 %copy-start = (bf16[9,32]{1,0:T(8,128)(2,1)S(1)}, bf16[9,32]{1,0:T(8,128)(2,1)}, u32[]{:S(2)}) copy-start(bf16[9,32]{1,0:T(8,128)(2,1)} %param.20) | copy-start | bytes 1732
where the time goes:
time: 138 us; the launch traced here: 137 us
  Pallas kernels  117 us (85%)
  local copies, waits for them, and re-layouts  13.9 us (10%)
  other arithmetic  4.2 us (3%)
  between operations  2.51 us (2%)
    pallas_call x1, Pallas kernels, body(): pl.pallas_call(functools.partial(plane_kernel, modes), grid=(planes,), ou...  44.8 us
    pallas_call x3, Pallas kernels, exchange(): pl.pallas_call(functools.partial(exchange_kernel, 'px', devices, count),...  44.5 us
    pallas_call x1, Pallas kernels, body(): pl.pallas_call(functools.partial(lift_kernel, modes), grid=(planes,), out...  11.3 us
    mul x10, local copies, waits for them, and re-layouts, spread(): out = weight[:, None, :, None] * eye[None, :, None, :]  9.51 us
    pallas_call x1, Pallas kernels, body(): pl.pallas_call(adam_kernel, grid=(quads,), out_shape=(jax.ShapeDtypeStruc...  9.44 us
    pallas_call x1, Pallas kernels, body(): pl.pallas_call(mix_kernel, grid=(quads,), out_shape=(jax.ShapeDtypeStruct...  6.78 us

commit v1 on v0

--- a/solution.py
+++ b/solution.py
@@ -76,12 +76,13 @@
 
 def table_dot(table, data):
     high, low = parts_of(data)
-    return dot(table[0], high) + (dot(table[1], high) + dot(table[0], low))
+    t_high, t_low = table[0].astype(bf16), table[1].astype(bf16)
+    return dot(t_high, high) + (dot(t_low, high) + dot(t_high, low))
 
 
 def forward_yz(field_ref, zs_ref, z_fwd_ref, y_fwd_ref, out_ref, plane, modes):
     chans = field_ref.shape[0]
-    z_fwd = z_fwd_ref[...]
+    z_fwd = z_fwd_ref[...].astype(bf16)
 
     for c in range(chans):
         zs_ref[:, c, :] = dot_nt(z_fwd, field_ref[c])
@@ -89,7 +90,7 @@
     for part in range(2):
         data = zs_ref[pl.ds(part * modes, modes)].reshape(modes * chans, zs_ref.shape[2])
         high, low = parts_of(data)
-        t_high, t_low = y_fwd_ref[part, 0], y_fwd_ref[part, 1]
+        t_high, t_low = (y_fwd_ref[part, i].astype(bf16) for i in range(2))
         term = dot_nt(t_high, high) + (dot_nt(t_low, high) + dot_nt(t_high, low))
         total = term if total is None else total + term
     devices, _, slots, _ = out_ref.shape
@@ -112,8 +113,33 @@
                 ]
 
 
-def lift_kernel(modes, fields_ref, lift_ref, z_fwd_ref, y_fwd_ref, out_ref, field_ref, zs_ref):
+def spread(weight, table_refs, flip):
+    rows_ref, cols_ref, mask_ref = table_refs
+    rows, cols = rows_ref[...].astype(bf16), cols_ref[...].astype(bf16)
+    tall = dot_nt(rows, weight) if flip else dot(rows, weight)
+    return (dot(tall.astype(bf16), cols) * mask_ref[...]).astype(bf16)
+
+
+def lift_kernel(
+    modes,
+    fields_ref,
+    weight_ref,
+    rows_ref,
+    cols_ref,
+    mask_ref,
+    z_fwd_ref,
+    y_fwd_ref,
+    out_ref,
+    field_ref,
+    zs_ref,
+    lift_ref,
+):
     plane = pl.program_id(0)
+
+    @pl.when(plane == 0)
+    def _():
+        lift_ref[...] = spread(weight_ref[...], (rows_ref, cols_ref, mask_ref), True)
+
     grid_y, grid_z = fields_ref.shape[2:]
     chans = field_ref.shape[0]
 
@@ -147,7 +173,8 @@
 
 def expand(data, e_ref):
     high, low = parts_of(spread_rows(data))
-    return dot(high, e_ref[...]) + dot(low, e_ref[...])
+    table = e_ref[...].astype(bf16)
+    return dot(high, table) + dot(low, table)
 
 
 def mix_kernel(recv_ref, weight_ref, x_fwd_ref, x_inv_ref, e_ref, vhat_ref, out_ref):
@@ -190,7 +217,9 @@
 
 def gelu_parts(u):
     e = jnp.exp(u * u * -0.5)
-    t = 1.0 / (1.0 + (poly_p / math.sqrt(2.0)) * jnp.abs(u))
+    d = 1.0 + (poly_p / math.sqrt(2.0)) * jnp.abs(u)
+    t = pl.reciprocal(d, approx=True)
+    t = t * (2.0 - d * t)
     q = 0.5 * poly[4]
     for a in poly[3::-1]:
         q = q * t + 0.5 * a
@@ -204,12 +233,21 @@
     recv_ref,
     fields_ref,
     target_ref,
-    lift_ref,
-    mix_ref,
-    bias_ref,
-    proj_ref,
-    proj_t_ref,
-    proj_bias_ref,
+    lift_weight_ref,
+    mix_weight_ref,
+    mix_bias_ref,
+    proj_weight_ref,
+    comp_bias_ref,
+    lift_rows_ref,
+    lift_cols_ref,
+    lift_mask_ref,
+    chan_rows_ref,
+    chan_cols_ref,
+    chan_mask_ref,
+    comp_rows_ref,
+    comp_cols_ref,
+    down_mask_ref,
+    up_mask_ref,
     z_fwd_ref,
     z_rep_ref,
     y_fwd_ref,
@@ -221,8 +259,31 @@
     zs_ref,
     us_ref,
     v_ref,
+    lift_ref,
+    mix_ref,
+    proj_ref,
+    proj_t_ref,
+    bias_ref,
+    proj_bias_ref,
 ):
     plane = pl.program_id(0)
+
+    @pl.when(plane == 0)
+    def _():
+        proj = proj_weight_ref[...]
+        lift_ref[...] = spread(
+            lift_weight_ref[...], (lift_rows_ref, lift_cols_ref, lift_mask_ref), True
+        )
+        mix_ref[...] = spread(
+            mix_weight_ref[...], (chan_rows_ref, chan_cols_ref, chan_mask_ref), True
+        )
+        proj_ref[...] = spread(proj, (comp_rows_ref, chan_cols_ref, down_mask_ref), True)
+        proj_t_ref[...] = spread(proj, (chan_rows_ref, comp_cols_ref, up_mask_ref), False)
+        for c in range(bias_ref.shape[0]):
+            bias_ref[c] = jnp.full(bias_ref.shape[1:], mix_bias_ref[c], f32)
+        for c in range(proj_bias_ref.shape[0]):
+            proj_bias_ref[c] = jnp.full(proj_bias_ref.shape[1:], comp_bias_ref[c], f32)
+
     grid_y, grid_z = fields_ref.shape[2:]
     chans = field_ref.shape[0]
     comps = target_ref.shape[0]
@@ -246,7 +307,8 @@
         )
     spec = jnp.concatenate(columns, 1).T
     high, low = parts_of(spec)
-    t_high, t_low = y_inv_ref[0], y_inv_ref[1]
+    t_high, t_low = (y_inv_ref[i].astype(bf16) for i in range(2))
+    z_rep = z_rep_ref[...].astype(bf16)
     u = dot(high, t_high) + (dot(high, t_low) + dot(low, t_high))
     us_ref[...] = u.reshape(modes, chans, 2 * grid_y)
     for o in range(chans):
@@ -261,7 +323,7 @@
         at = pl.ds(pl.multiple_of(i * 16, 16), 16)
         data = fields_ref[:, 0, at, :].reshape(-1, grid_z)
         lifted = dot(lift_ref[...], data).astype(bf16)
-        spatial = dot(v_ref[:, at, :].reshape(chans * 16, -1), z_rep_ref[...])
+        spatial = dot(v_ref[:, at, :].reshape(chans * 16, -1), z_rep)
         spatial = spatial.reshape(chans, 16, grid_z)
         target = target_ref[:, 0, at, :].astype(f32)
         stress, grads = [], []
@@ -300,11 +362,30 @@
 
 
 def adam_kernel(
-    recv_ref, vhat_ref, scale_ref, first_ref, second_ref, x_ref, e_ref, f_ref, first_out, step_out
+    axis,
+    cells,
+    recv_ref,
+    vhat_ref,
+    errors_ref,
+    first_ref,
+    second_ref,
+    x_ref,
+    e_ref,
+    f_ref,
+    loss_out,
+    first_out,
+    step_out,
 ):
     quad = pl.program_id(0)
+
+    @pl.when(quad == 0)
+    def _():
+        loss_out[0] = jnp.sum(jnp.sum(errors_ref[...], 0)) / cells
+
     d_real, d_imag = forward_x(recv_ref, x_ref, quad)
-    scale = scale_ref[0]
+    pairs = 2 * recv_ref.shape[1]
+    pair = lax.axis_index(axis) * pairs + quad * 4 + lane_group((1, 128))
+    scale = jnp.where(pair < d_real.shape[0], 1.0, 2.0)
     b_real, b_imag = expand(d_real * scale, f_ref), expand(d_imag * scale, f_ref)
     a_real, a_imag = expand(vhat_ref[0, 0], e_ref), expand(vhat_ref[0, 1], e_ref)
     half = d_real.shape[0]
@@ -403,10 +484,20 @@
     return pl.BlockSpec(tuple(shape), lambda i: zeros)
 
 
-def spread(weight, size):
-    eye = jnp.eye(size, dtype=weight.dtype)
-    out = weight[:, None, :, None] * eye[None, :, None, :]
-    return out.reshape(weight.shape[0] * size, weight.shape[1] * size)
+def spread_tables(rows, cols, size, halves=1):
+    inner = size // halves
+    row_y = np.tile(np.arange(inner), rows)
+    row_y = np.concatenate([row_y + h * inner for h in range(halves)])
+    row_of = np.tile(np.repeat(np.arange(rows), inner), halves)
+    col_of, col_y = np.repeat(np.arange(cols), size), np.tile(np.arange(size), cols)
+    return tuple(
+        jnp.asarray(t.astype(np.float32))
+        for t in (
+            row_of[:, None] == np.arange(rows)[None, :],
+            np.arange(cols)[:, None] == col_of[None, :],
+            row_y[:, None] == col_y[None, :],
+        )
+    )
 
 
 def body(
@@ -422,7 +513,6 @@
     second_moment,
 ):
     devices = lax.axis_size("px")
-    rank = lax.axis_index("px")
     in_ch, planes, grid_y, grid_z = fields.shape
     chans = mix_weight.shape[0]
     comps = target.shape[0]
@@ -433,23 +523,22 @@
     quads = local_pairs // 4
     slots = 2 * quads
     z_fwd, z_rep, y_fwd, y_inv, x_fwd, x_inv = (
-        jnp.asarray(t) for t in make_tables(modes, grid_x, grid_y, grid_z)
+        jnp.asarray(t.astype(np.float32)) for t in make_tables(modes, grid_x, grid_y, grid_z)
     )
     lanes = np.arange(128) % 32
-    e_table = jnp.asarray((lanes[:, None] == np.arange(1024)[None, :] // 32).astype(bf16))
-    f_table = jnp.asarray((lanes[:, None] == lanes[None, :]).astype(bf16))
+    e_table = jnp.asarray((lanes[:, None] == np.arange(1024)[None, :] // 32).astype(np.float32))
+    f_table = jnp.asarray((lanes[:, None] == lanes[None, :]).astype(np.float32))
     chunk = (devices, planes, slots, 128)
     params = pltpu.CompilerParams(
         dimension_semantics=("arbitrary",), vmem_limit_bytes=vmem_limit
     )
 
-    lift16 = spread(lift_weight.T, 16)
-    lift_split = (
-        lift16.reshape(chans, 2, 8, in_ch * 16).transpose(1, 0, 2, 3).reshape(chans * 16, -1)
-    )
-    mix8 = spread(mix_weight.T, 8)
-    proj8 = spread(proj_weight.T, 8)
-    proj8_t = spread(proj_weight, 8)
+    lift_rows, lift_cols, lift_mask = spread_tables(chans, in_ch, 16)
+    split_rows, split_cols, split_mask = spread_tables(chans, in_ch, 16, 2)
+    chan_rows, chan_cols, chan_mask = spread_tables(chans, chans, 8)
+    comp_rows, _, down_mask = spread_tables(comps, chans, 8)
+    _, comp_cols, up_mask = spread_tables(chans, comps, 8)
+    smem = pl.BlockSpec(memory_space=pltpu.SMEM)
 
     plane_block = lambda n: pl.BlockSpec((n, 1, grid_y, grid_z), lambda p: (0, p, 0, 0))
     spectra = pl.pallas_call(
@@ -458,7 +547,10 @@
         out_shape=jax.ShapeDtypeStruct(chunk, f32),
         in_specs=[
             plane_block(in_ch),
-            whole(lift16.shape),
+            whole(lift_weight.shape),
+            whole(lift_rows.shape),
+            whole(lift_cols.shape),
+            whole(lift_mask.shape),
             whole(z_fwd.shape),
             whole(y_fwd.shape),
         ],
@@ -466,10 +558,11 @@
         scratch_shapes=[
             pltpu.VMEM((chans, grid_y, grid_z), bf16),
             pltpu.VMEM((half, chans, grid_y), f32),
+            pltpu.VMEM(lift_mask.shape, bf16),
         ],
         compiler_params=params,
         name="lift_spectrum",
-    )(fields, lift16, z_fwd, y_fwd)
+    )(fields, lift_weight, lift_rows, lift_cols, lift_mask, z_fwd, y_fwd)
 
     (moved,) = exchange([spectra], devices, 0)
 
@@ -497,8 +590,10 @@
 
     (result,) = exchange([sending.reshape(chunk)], devices, 1)
 
-    bias = jnp.broadcast_to(mix_bias[:, None, None], (chans, 1, grid_z))
-    pbias = jnp.broadcast_to(proj_bias[:, None, None], (comps, 1, grid_z))
+    tables = (
+        split_rows, split_cols, split_mask, chan_rows, chan_cols, chan_mask,
+        comp_rows, comp_cols, down_mask, up_mask, z_fwd, z_rep, y_fwd, y_inv,
+    )
     stress, grad_spectra, err = pl.pallas_call(
         functools.partial(plane_kernel, modes),
         grid=(planes,),
@@ -508,54 +603,54 @@
             jax.ShapeDtypeStruct((8, 128), f32),
         ),
         in_specs=[whole(chunk), plane_block(in_ch), plane_block(comps)]
-        + [
-            whole(a.shape)
-            for a in (
-                lift_split, mix8, bias, proj8, proj8_t, pbias, z_fwd, z_rep, y_fwd, y_inv
-            )
-        ],
+        + [whole(lift_weight.shape), whole(mix_weight.shape), smem]
+        + [whole(proj_weight.shape), smem]
+        + [whole(a.shape) for a in tables],
         out_specs=(plane_block(comps), whole(chunk), whole((8, 128))),
         scratch_shapes=[
             pltpu.VMEM((chans, grid_y, grid_z), bf16),
             pltpu.VMEM((half, chans, grid_y), f32),
             pltpu.VMEM((modes, chans, 2 * grid_y), f32),
             pltpu.VMEM((chans, grid_y, 8 * modes), bf16),
+            pltpu.VMEM(split_mask.shape, bf16),
+            pltpu.VMEM(chan_mask.shape, bf16),
+            pltpu.VMEM(down_mask.shape, bf16),
+            pltpu.VMEM(up_mask.shape, bf16),
+            pltpu.VMEM((chans, 1, grid_z), f32),
+            pltpu.VMEM((comps, 1, grid_z), f32),
         ],
         compiler_params=params,
         name="planes",
     )(
-        result, fields, target, lift_split, mix8, bias, proj8, proj8_t, pbias,
-        z_fwd, z_rep, y_fwd, y_inv,
+        result, fields, target, lift_weight, mix_weight, mix_bias, proj_weight, proj_bias,
+        *tables,
     )
 
     grads_moved, errors = exchange([grad_spectra, err], devices, 2)
-    loss = (jnp.sum(errors) / (2.0 * comps * grid_x * grid_y * grid_z)).reshape(1)
-
-    kz_index = (rank * local_pairs + jnp.arange(local_pairs, dtype=jnp.int32)) // half
-    scale = jnp.where(kz_index == 0, 1.0, 2.0).astype(f32)
-    scale = jnp.repeat(scale, 32).reshape(quads, 1, 128)
-    first_new, step = pl.pallas_call(
-        adam_kernel,
+    cells = 2.0 * comps * grid_x * grid_y * grid_z
+    loss, first_new, step = pl.pallas_call(
+        functools.partial(adam_kernel, "px", cells),
         grid=(quads,),
         out_shape=(
+            jax.ShapeDtypeStruct((1,), f32),
             jax.ShapeDtypeStruct(first_moment.shape, f32),
             jax.ShapeDtypeStruct(first_moment.shape, f32),
         ),
         in_specs=[
             whole(flat),
             vhat_block,
-            pl.BlockSpec((1, 1, 128), lambda q: (q, 0, 0)),
+            whole(errors.shape),
             pair_block,
             pair_block,
             whole(x_fwd.shape),
             whole(e_table.shape),
             whole(f_table.shape),
         ],
-        out_specs=(pair_block, pair_block),
+        out_specs=(smem, pair_block, pair_block),
         compiler_params=params,
         name="adam",
     )(
-        grads_moved.reshape(flat), vhat, scale, first_moment, second_moment,
+        grads_moved.reshape(flat), vhat, errors, first_moment, second_moment,
         x_fwd, e_table, f_table,
     )
     return (stress, loss, first_new, step)

time: 138 us -> 123 us (0.89)
  local copies, waits for them, and re-layouts: 13.9 us -> 1.37 us
  other arithmetic: 4.2 us -> 0 us
  Pallas kernels: 117 us -> 121 us
  between operations: 2.51 us -> 0.66 us
    mul x10 -> x0, local copies, waits for them, and re-layouts: 9.51 us -> none  [spread(): out = weight[:, None, :, None] * eye[None, :, None, :]]
    broadcast_in_dim x4 -> x0, local copies, waits for them, and re-layouts: 3.44 us -> none  [the longest x1 1.37 us: body(): bias = jnp.broadcast_to(mix_bias[:, None, None], (chans, 1, grid_z))]
    pallas_call x1, Pallas kernels: 44.8 us -> 48.1 us  [body(): pl.pallas_call(functools.partial(plane_kernel, modes), grid=(planes,), ou...]
    mul x5 -> x0, other arithmetic: 2.63 us -> none  [spread(): out = weight[:, None, :, None] * eye[None, :, None, :]]
    reduce_sum x1 -> x0, other arithmetic: 1.54 us -> none  [body(): jnp.sum(errors) / (2.0 * comps * grid_x * grid_y * grid_z)]
where the time goes in v1:
time: 123 us
  Pallas kernels  121 us (98%)
  local copies, waits for them, and re-layouts  1.37 us (1%)
    pallas_call x1, Pallas kernels, body(): pl.pallas_call(functools.partial(plane_kernel, modes), grid=(planes,), ou...  48.1 us
    pallas_call x3, Pallas kernels, exchange(): pl.pallas_call(functools.partial(exchange_kernel, 'px', devices, count),...  44.5 us
    pallas_call x1, Pallas kernels, body(): pl.pallas_call(functools.partial(lift_kernel, modes), grid=(planes,), out...  11.9 us
    pallas_call x1, Pallas kernels, body(): pl.pallas_call(functools.partial(adam_kernel, 'px', cells), grid=(quads,)...  9.64 us
    pallas_call x1, Pallas kernels, body(): pl.pallas_call(mix_kernel, grid=(quads,), out_shape=(jax.ShapeDtypeStruct...  6.9 us

profile of v1, /device:TPU:15, one launch (start us, length us, event | category | flops | bytes accessed | tf_op | source)
XLA Modules:
  0.0 123.1 jit_solution(2021985929815691180)
XLA Ops:
  0.6 1.4 %copy.35.proj_weight_ref = bf16[32,6]{1,0:T(8,128)(2,1)} copy(bf16[32,6]{0,1:T(8,128)(2,1)} %param.36) | data formatting | bytes 768 | tf_op args[5]
  2.0 11.9 %lift_spectrum.1.refs_0_ = f32[32,2,8,128]{3,2,1,0:T(8,128)} custom-call(bf16[9,2,256,256]{3,2,1,0:T(8,128)(2,1)} %fields_ref.3, bf16[9,32]{1,0:T(8,128)(2,1)} %lift_weight_ref.1, f32[512,32]{1,0:T(8,128)} %constant.48.clone.rows_ref, f32[9,144]{1,0:T(8,128)} %constant.49.clone.cols_ref.lift_cols_ref, f32[512,144]{1,0:T(8,128)} %constant.50.clone.mask_ref, ...), custom_call_target="tpu_custom_call" | custom-call | tf_op jit(solution)/shard_map/lift_spectrum/pallas_call | solution.py:544
  13.9 14.0 %exchange0.1 = f32[32,2,8,128]{3,2,1,0:T(8,128)} custom-call(f32[32,2,8,128]{3,2,1,0:T(8,128)} %lift_spectrum.1.refs_0_), custom_call_target="tpu_custom_call" | custom-call | tf_op jit(solution)/shard_map/exchange0/pallas_call | solution.py:467
  27.9 6.9 %mix_modes.1 = (f32[4,2,32,128]{3,2,1,0:T(8,128)}, f32[64,8,128]{2,1,0:T(8,128)}) custom-call(f32[64,8,128]{2,1,0:T(8,128)} %bitcast.3, f32[2,16,32,1024]{3,2,1,0:T(8,128)} %weight_ref.3, f32[2,64,64]{2,1,0:T(8,128)} %constant.44.clone.x_fwd_ref.x_ref, f32[2,128,64]{2,1,0:T(8,128)} %constant.45.clone.x_inv_ref, f32[128,1024]{1,0:T(8,128)} %constant.46.clone.e_ref), custom_call_target="tpu_custom_call" | custom-call | tf_op jit(solution)/shard_map/mix_modes/pallas_call | solution.py:572
  34.8 13.5 %exchange1.1.recv_ref = f32[32,2,8,128]{3,2,1,0:T(8,128)} custom-call(f32[32,2,8,128]{3,2,1,0:T(8,128)} %bitcast.5), custom_call_target="tpu_custom_call" | custom-call | tf_op jit(solution)/shard_map/exchange1/pallas_call | solution.py:467
  48.3 48.1 %planes.1 = (bf16[6,2,256,256]{3,2,1,0:T(8,128)(2,1)}, f32[32,2,8,128]{3,2,1,0:T(8,128)}, f32[8,128]{1,0:T(8,128)}) custom-call(f32[32,2,8,128]{3,2,1,0:T(8,128)} %exchange1.1.recv_ref, bf16[9,2,256,256]{3,2,1,0:T(8,128)(2,1)} %fields_ref.3, bf16[6,2,256,256]{3,2,1,0:T(8,128)(2,1)} %target_ref.1, bf16[9,32]{1,0:T(8,128)(2,1)} %lift_weight_ref.1, ...), custom_call_target="tpu_custom_call" | custom-call | tf_op jit(solution)/shard_map/planes/pallas_call | solution.py:597
  96.4 17.0 %exchange2.1 = (f32[32,2,8,128]{3,2,1,0:T(8,128)}, f32[32,8,128]{2,1,0:T(8,128)}) custom-call(f32[32,2,8,128]{3,2,1,0:T(8,128)} %get-tuple-element.16.refs_0_, f32[8,128]{1,0:T(8,128)} %get-tuple-element.17.refs_1_), custom_call_target="tpu_custom_call" | custom-call | tf_op jit(solution)/shard_map/exchange2/pallas_call | solution.py:467
  113.4 9.6 %adam.1 = (f32[1]{0:T(128)}, f32[2,16,32,1024]{3,2,1,0:T(8,128)}, f32[2,16,32,1024]{3,2,1,0:T(8,128)}) custom-call(f32[64,8,128]{2,1,0:T(8,128)} %bitcast.4, f32[4,2,32,128]{3,2,1,0:T(8,128)} %get-tuple-element.19.vhat_ref, f32[32,8,128]{2,1,0:T(8,128)} %get-tuple-element.20.errors_ref, f32[2,16,32,1024]{3,2,1,0:T(8,128)} %first_ref.1, ...), custom_call_target="tpu_custom_call" | custom-call | tf_op jit(solution)/shard_map/adam/pallas_call | solution.py:631

commit v2 on v1

--- a/solution.py
+++ b/solution.py
@@ -345,7 +345,7 @@
         field_ref[:, at, :] = jnp.concatenate(grads, 1).astype(bf16)
         return err
 
-    err = lax.fori_loop(0, grid_y // 16, step, jnp.zeros((8, grid_z), f32))
+    err = lax.fori_loop(0, grid_y // 16, step, jnp.zeros((8, grid_z), f32), unroll=2)
     folded = err[:, :128]
     for t in range(1, grid_z // 128):
         folded = folded + err[:, t * 128 : (t + 1) * 128]

time: 123 us -> 120 us (0.976)
  Pallas kernels: 121 us -> 117 us
    pallas_call x1, Pallas kernels: 48.1 us -> 44.2 us  [body(): pl.pallas_call(functools.partial(plane_kernel, modes), grid=(planes,), ou...]
where the time goes in v2:
time: 120 us; the launch traced here: 119 us
  Pallas kernels  117 us (98%)
  local copies, waits for them, and re-layouts  1.37 us (1%)
    pallas_call x3, Pallas kernels, exchange(): pl.pallas_call(functools.partial(exchange_kernel, 'px', devices, count),...  44.5 us
    pallas_call x1, Pallas kernels, body(): pl.pallas_call(functools.partial(plane_kernel, modes), grid=(planes,), ou...  44.2 us
    pallas_call x1, Pallas kernels, body(): pl.pallas_call(functools.partial(lift_kernel, modes), grid=(planes,), out...  11.9 us
    pallas_call x1, Pallas kernels, body(): pl.pallas_call(functools.partial(adam_kernel, 'px', cells), grid=(quads,)...  9.64 us
    pallas_call x1, Pallas kernels, body(): pl.pallas_call(mix_kernel, grid=(quads,), out_shape=(jax.ShapeDtypeStruct...  6.9 us

profile of v2, /device:TPU:15, one launch (start us, length us, event | category | flops | bytes accessed | tf_op | source)
XLA Modules:
  0.0 119.2 jit_solution(9999334825463905740)
XLA Ops:
  0.6 1.4 %copy.35.proj_weight_ref = bf16[32,6]{1,0:T(8,128)(2,1)} copy(bf16[32,6]{0,1:T(8,128)(2,1)} %param.36) | data formatting | bytes 768 | tf_op args[5]
  2.0 11.9 %lift_spectrum.1.refs_0_ = f32[32,2,8,128]{3,2,1,0:T(8,128)} custom-call(bf16[9,2,256,256]{3,2,1,0:T(8,128)(2,1)} %fields_ref.3, bf16[9,32]{1,0:T(8,128)(2,1)} %lift_weight_ref.1, f32[512,32]{1,0:T(8,128)} %constant.48.clone.rows_ref, f32[9,144]{1,0:T(8,128)} %constant.49.clone.cols_ref.lift_cols_ref, f32[512,144]{1,0:T(8,128)} %constant.50.clone.mask_ref, ...), custom_call_target="tpu_custom_call" | custom-call | tf_op jit(solution)/shard_map/lift_spectrum/pallas_call | solution.py:544
  13.9 14.0 %exchange0.1 = f32[32,2,8,128]{3,2,1,0:T(8,128)} custom-call(f32[32,2,8,128]{3,2,1,0:T(8,128)} %lift_spectrum.1.refs_0_), custom_call_target="tpu_custom_call" | custom-call | tf_op jit(solution)/shard_map/exchange0/pallas_call | solution.py:467
  27.9 6.9 %mix_modes.1 = (f32[4,2,32,128]{3,2,1,0:T(8,128)}, f32[64,8,128]{2,1,0:T(8,128)}) custom-call(f32[64,8,128]{2,1,0:T(8,128)} %bitcast.3, f32[2,16,32,1024]{3,2,1,0:T(8,128)} %weight_ref.3, f32[2,64,64]{2,1,0:T(8,128)} %constant.44.clone.x_fwd_ref.x_ref, f32[2,128,64]{2,1,0:T(8,128)} %constant.45.clone.x_inv_ref, f32[128,1024]{1,0:T(8,128)} %constant.46.clone.e_ref), custom_call_target="tpu_custom_call" | custom-call | tf_op jit(solution)/shard_map/mix_modes/pallas_call | solution.py:572
  34.8 13.5 %exchange1.1.recv_ref = f32[32,2,8,128]{3,2,1,0:T(8,128)} custom-call(f32[32,2,8,128]{3,2,1,0:T(8,128)} %bitcast.5), custom_call_target="tpu_custom_call" | custom-call | tf_op jit(solution)/shard_map/exchange1/pallas_call | solution.py:467
  48.3 44.2 %planes.1 = (bf16[6,2,256,256]{3,2,1,0:T(8,128)(2,1)}, f32[32,2,8,128]{3,2,1,0:T(8,128)}, f32[8,128]{1,0:T(8,128)}) custom-call(f32[32,2,8,128]{3,2,1,0:T(8,128)} %exchange1.1.recv_ref, bf16[9,2,256,256]{3,2,1,0:T(8,128)(2,1)} %fields_ref.3, bf16[6,2,256,256]{3,2,1,0:T(8,128)(2,1)} %target_ref.1, bf16[9,32]{1,0:T(8,128)(2,1)} %lift_weight_ref.1, ...), custom_call_target="tpu_custom_call" | custom-call | tf_op jit(solution)/shard_map/planes/pallas_call | solution.py:597
  92.5 17.0 %exchange2.1 = (f32[32,2,8,128]{3,2,1,0:T(8,128)}, f32[32,8,128]{2,1,0:T(8,128)}) custom-call(f32[32,2,8,128]{3,2,1,0:T(8,128)} %get-tuple-element.16.refs_0_, f32[8,128]{1,0:T(8,128)} %get-tuple-element.17.refs_1_), custom_call_target="tpu_custom_call" | custom-call | tf_op jit(solution)/shard_map/exchange2/pallas_call | solution.py:467
  109.6 9.6 %adam.1 = (f32[1]{0:T(128)}, f32[2,16,32,1024]{3,2,1,0:T(8,128)}, f32[2,16,32,1024]{3,2,1,0:T(8,128)}) custom-call(f32[64,8,128]{2,1,0:T(8,128)} %bitcast.4, f32[4,2,32,128]{3,2,1,0:T(8,128)} %get-tuple-element.19.vhat_ref, f32[32,8,128]{2,1,0:T(8,128)} %get-tuple-element.20.errors_ref, f32[2,16,32,1024]{3,2,1,0:T(8,128)} %first_ref.1, ...), custom_call_target="tpu_custom_call" | custom-call | tf_op jit(solution)/shard_map/adam/pallas_call | solution.py:631
